TPU v7x, 32 devices: a whole 2x2x4 slice. The times are simulated.
32 devices in a mesh: groups: 2 (over x), row: 16 (over z, y, core).
Axes of the slice: x: 2, y: 2, z: 4, core: 2. Of those that a mesh axis runs over, the one named last changes fastest.
Arguments:
- features: bfloat16 [64, 256, 512], P(('groups', 'row')), parts along dimension 0, may hold values from -6 to 6
- labels: int32 [64, 256], P(('groups', 'row')), parts along dimension 0, may hold values from 0 to 7
- kernel_one: bfloat16 [3, 3, 512, 512], replicated, may hold values from -0.09375 to 0.09375
- kernel_two: bfloat16 [3, 3, 512, 512], replicated, may hold values from -0.09375 to 0.09375
- head_weight: bfloat16 [512, 8], replicated, may hold values from -1 to 1
Outputs:
- section_out: bfloat16 [64, 256, 512], P(('groups', 'row')), parts along dimension 0
- grad_one: float32 [1024, 3, 3, 512], P(('groups', 'row')), parts along dimension 0
- grad_two: float32 [1024, 3, 3, 512], P(('groups', 'row')), parts along dimension 0
- grad_head: float32 [1024, 8], P(('groups', 'row')), parts along dimension 0
There are 2 independent parts, one for each index of `groups`. A program takes and returns all parts, laid end to end along the dimension named above; an argument that names none is the same for every part. Nothing has to cross between parts.
All inputs are finite; a program needn't handle non-finite values.
Results may differ from a plain program's by a relative error of at most 0.019.
The roundings to bfloat16 on the way count: a program that leaves them out, or rounds other values in their place, can miss the bound.
Values may be sent and summed in bfloat16 or wider, within the bound.
A program may use at most 128 MiB of HBM per device.

v0:
```python
import jax
import jax.numpy as jnp
from jax import lax
from jax.sharding import PartitionSpec as P


def extended(block, sides, width):
    for axis, dim in sides:
        count = lax.axis_size(axis)
        forward = [(i, i + 1) for i in range(count - 1)]
        backward = [(target, source) for source, target in forward]
        low = lax.ppermute(
            lax.slice_in_dim(block, block.shape[dim] - width, None, axis=dim), axis, forward
        )
        high = lax.ppermute(lax.slice_in_dim(block, 0, width, axis=dim), axis, backward)
        block = jnp.concatenate([low, block, high], axis=dim)
    return block


def gather_taps(padded_rows, out_rows):
    width = padded_rows.shape[1]
    chans = padded_rows.shape[2]
    padded = jnp.pad(padded_rows, ((0, 0), (1, 1), (0, 0)))
    pieces = []
    for tap_a in range(3):
        for tap_b in range(3):
            pieces.append(padded[tap_a : tap_a + out_rows, tap_b : tap_b + width])
    stacked = jnp.stack(pieces, axis=2)
    return stacked.reshape(out_rows * width, 9, chans)


def apply_kernel(tap_values, kernel):
    pixels = tap_values.shape[0]
    chans = tap_values.shape[2]
    return jnp.dot(
        tap_values.reshape(pixels, 9 * chans),
        kernel.reshape(9 * chans, kernel.shape[3]),
        preferred_element_type=jnp.float32,
    )


def grad_term(tap_values, cotan_flat):
    chans = tap_values.shape[2]
    term = jnp.einsum("ptc,pd->ctd", tap_values, cotan_flat, preferred_element_type=jnp.float32)
    return term.reshape(chans, 3, 3, cotan_flat.shape[1])


def per_device(features, labels, kernel_one, kernel_two, head_weight):
    rows, width, chans = features.shape
    pixels = rows * width
    devices = lax.axis_size("row")
    deep_rows = extended(features, (("row", 0),), 2)
    big_taps = gather_taps(deep_rows, rows + 2)
    big_hidden = (
        jnp.maximum(apply_kernel(big_taps, kernel_one), 0.0)
        .astype(jnp.bfloat16)
        .reshape(rows + 2, width, chans)
    )
    global_row = lax.axis_index("row") * rows - 1 + jnp.arange(rows + 2, dtype=jnp.int32)
    inside = (global_row >= 0) & (global_row < rows * devices)
    hidden_rows = jnp.where(inside[:, None, None], big_hidden, jnp.zeros_like(big_hidden))
    hidden = hidden_rows[1 : rows + 1]
    input_taps = big_taps.reshape(rows + 2, width, 9, chans)[1 : rows + 1].reshape(pixels, 9, chans)
    hidden_taps = gather_taps(hidden_rows, rows)
    section_out = jnp.maximum(apply_kernel(hidden_taps, kernel_two), 0.0).astype(jnp.bfloat16)
    logits = jnp.dot(section_out, head_weight, preferred_element_type=jnp.float32)
    classes = head_weight.shape[1]
    onehot = (labels.reshape(-1)[:, None] == jnp.arange(classes, dtype=jnp.int32)[None, :]).astype(
        jnp.float32
    )
    scale = 1.0 / jnp.sqrt(jnp.float32(rows * devices * width))
    dlogits = ((logits - onehot) * scale).astype(jnp.bfloat16)
    head_term = lax.dot_general(
        section_out, dlogits, (((0,), (0,)), ((), ())), preferred_element_type=jnp.float32
    )
    dout_full = lax.dot_general(
        dlogits, head_weight, (((1,), (1,)), ((), ())), preferred_element_type=jnp.float32
    )
    dout = (dout_full * (section_out > 0).astype(jnp.float32)).astype(jnp.bfloat16)
    dout_rows = extended(dout.reshape(rows, width, chans), (("row", 0),), 1)
    dout_taps = gather_taps(dout_rows, rows)
    flipped = kernel_two[::-1, ::-1].reshape(9, chans, chans)
    dhidden_full = lax.dot_general(
        dout_taps, flipped, (((1, 2), (0, 2)), ((), ())), preferred_element_type=jnp.float32
    )
    dhidden = (dhidden_full * (hidden.reshape(pixels, chans) > 0).astype(jnp.float32)).astype(
        jnp.bfloat16
    )
    one_term = grad_term(input_taps, dhidden)
    two_term = grad_term(hidden_taps, dout)
    grad_one, grad_two, grad_head = (
        lax.psum_scatter(one_term, "row", scatter_dimension=0, tiled=True),
        lax.psum_scatter(two_term, "row", scatter_dimension=0, tiled=True),
        lax.psum_scatter(head_term, "row", scatter_dimension=0, tiled=True),
    )
    return (section_out.reshape(rows, width, chans), grad_one, grad_two, grad_head)


def solution(mesh):
    placed = (P(("groups", "row"), None, None), P(("groups", "row"), None), P(), P(), P())
    return jax.shard_map(
        per_device,
        mesh=mesh,
        in_specs=placed,
        out_specs=(
            P(("groups", "row"), None, None),
            P(("groups", "row"), None, None, None),
            P(("groups", "row"), None, None, None),
            P(("groups", "row"), None),
        ),
        check_vma=False,
    )
```

profile of v0, /device:TPU:0, one launch (start us, length us, event | category | flops | bytes accessed | tf_op | source)
XLA Modules:
  0.0 406.3 jit_solution(1180446497771200761)
XLA Ops:
  7.2 2.5 collective-permute-start
  9.8 1.3 collective-permute-start.1
  11.8 1.1 constant_dynamic-update-slice_fusion.1
  12.9 3.0 collective-permute-done.1
  15.9 1.2 bitcast_dynamic-update-slice_fusion.5
  17.2 1.1 fusion.14
  18.2 1.2 bitcast_dynamic-update-slice_fusion.4
  19.5 1.3 bitcast_dynamic-update-slice_fusion.3
  20.7 1.0 fusion.13
  21.8 1.3 bitcast_dynamic-update-slice_fusion.2
  23.0 1.2 bitcast_dynamic-update-slice_fusion.1
  24.3 1.1 fusion.15
  25.4 1.3 bitcast_dynamic-update-slice_fusion
  26.7 15.2 %copy.29 = bf16[4,256,9,512]{1,0,3,2:T(4,128)(2,1)} copy(bf16[4,256,9,512]{3,1,0,2:T(8,128)(2,1)} %bitcast_dynamic-update-slice_fusion) | data formatting | bytes 18874368 | tf_op jit(solution)/shard_map/stack | solution.py:28
  41.8 10.5 %copy.51 = bf16[576,8,4,256]{3,1,2,0:T(8,128)(2,1)} copy(bf16[576,8,4,256]{3,2,1,0:T(4,128)(2,1)} %bitcast.124) | data formatting | bytes 18874368
  52.3 9.0 %maximum_convert_fusion = bf16[1024,512]{1,0:T(8,128)(2,1)S(1)} fusion(bf16[1024,4608]{0,1:T(8,128)(2,1)} %bitcast.128, bf16[4608,512]{1,0:T(8,128)(2,1)} %bitcast.158), kind=kOutput, calls=%fused_computation.3 | convolution fusion | flops 4832886784 | bytes 15204352 | tf_op jit(solution)/shard_map/dot_general | solution.py:35
  63.4 6.8 %pad_slice_fusion = (bf16[2,256,512]{1,0,2:T(2,128)(2,1)S(1)}, bf16[2,256,512]{1,0,2:T(2,128)(2,1)}, bf16[2,256,512]{1,0,2:T(2,128)(2,1)}, bf16[2,256,512]{1,0,2...) fusion(bf16[4,256,512]{1,0,2:T(4,128)(2,1)S(1)} %broadcast_sele, ...), kind=kLoop, calls=%fused_computation.33 | loop fusion | bytes 7340032 | tf_op jit(solution)/shard_map/slice | solution.py:27
  71.5 1.3 bitcast_dynamic-update-slice_fusion.12
  73.5 1.3 bitcast_dynamic-update-slice_fusion.10
  74.7 1.3 bitcast_dynamic-update-slice_fusion.9
  76.7 1.3 bitcast_dynamic-update-slice_fusion.7
  79.2 2.6 fusion.3
  82.6 1.0 fusion.22
  83.7 2.0 copy.34
  85.7 1.9 constant_dynamic-update-slice_fusion.19
  87.5 2.0 copy.35
  89.5 2.0 copy.36
  91.5 2.0 copy.37
  93.5 2.0 copy.38
  95.5 2.0 copy.39
  97.5 1.4 copy.40
  100.5 1.9 constant_dynamic-update-slice_fusion.18
  102.5 1.9 constant_dynamic-update-slice_fusion.17
  104.3 1.9 constant_dynamic-update-slice_fusion.16
  106.2 1.9 constant_dynamic-update-slice_fusion.15
  108.1 1.9 constant_dynamic-update-slice_fusion.14
  112.4 7.4 %fusion.17 = f32[512,9,512]{2,0,1:T(8,128)} fusion(bf16[512,9,512]{2,0,1:T(8,128)(2,1)} %constant_dynamic-update-slice_fusion.11, bf16[512,512]{1,0:T(8,128)(2,1)S(1)} %fusion.4), kind=kOutput, calls=%fused_computation.42 | convolution fusion | flops 2415919104 | bytes 14680064 | tf_op jit(solution)/shard_map/ptc,pd->ctd/dot_general | solution.py:44
  119.9 9.6 %copy.44 = f32[512,3,3,512]{3,0,2,1:T(8,128)} copy(f32[512,3,3,512]{0,3,2,1:T(8,128)} %bitcast.123) | data formatting | bytes 18874368 | tf_op jit(solution)/shard_map/reshape | solution.py:45
  129.6 4.8 %rev.3 = bf16[3,3,512,512]{3,2,1,0:T(8,128)(2,1)} reverse(bf16[3,3,512,512]{3,2,1,0:T(8,128)(2,1)} %param.8), dimensions={0,1} | reverse | bytes 9437184 | tf_op jit(solution)/shard_map/rev | solution.py:82
  134.4 4.9 %slice.145 = bf16[2,256,9,512]{3,1,0,2:T(8,128)(2,1)} slice(bf16[4,256,9,512]{3,1,0,2:T(8,128)(2,1)} %bitcast_dynamic-update-slice_fusion), slice={[1:3], [0:256], [0:9], [0:512]} | slice | bytes 9437184 | tf_op jit(solution)/shard_map/slice | solution.py:63
  139.3 1.3 collective-permute-start.3
  140.6 12.2 %collective-permute-start.2 = (bf16[1,256,512]{2,1,0:T(8,128)(2,1)S(1)}, bf16[1,256,512]{2,1,0:T(8,128)(2,1)S(1)}, u32[]{:S(2)}, u32[]{:S(2)}) collective-permute-start(bf16[1,256,512]{2,1,0:T(8,128)(2,1)S(1)} %get-tuple-element.21), channel_id=1, source_target_pairs={{0,1},{1,2},{2,3},{3,4},{4,5},{5,6},{6,7},{7,8},{8,9},{9,10},{10,1... | collective-permute-start | bytes 786440 | tf_op jit(solution)/shard_map/ppermute | solution.py:12
  155.6 2.1 copy-done.5
  157.7 14.0 %fusion.16 = f32[512,9,512]{2,0,1:T(8,128)} fusion(bf16[512,9,512]{2,0,1:T(8,128)(2,1)} %bitcast.134, pred[512,512]{1,0:T(32,128)(4,1)S(1)} %bitcast.155, bf16[512,9,512]{2,0,1:T(8,128)(2,1)} %copy-done.5, bf16[9,512,512]{2,1,0:T(8,128)(2,1)} %bitcast.133), kind=kOutput, calls=%fused_computation.39 | convolution fusion | flops 4832362496 | bytes 23855104 | tf_op jit(solution)/shard_map/ptc,pd->ctd/dot_general | solution.py:44
  171.7 9.7 %copy.33 = f32[512,3,3,512]{3,0,2,1:T(8,128)} copy(f32[512,3,3,512]{0,3,2,1:T(8,128)} %bitcast.127) | data formatting | bytes 18874368 | tf_op jit(solution)/shard_map/reshape | solution.py:45
  181.5 1.4 copy.50
  182.9 100.6 %reduce-scatter.8.cloned.1.call-done = f32[32,3,3,512]{3,0,2,1:T(8,128)} async-done(((f32[512,3,3,512]{3,0,2,1:T(8,128)}), f32[32,3,3,512]{3,0,2,1:T(8,128)}) %reduce-scatter.8.cloned.1.call-update) | async-done | bytes 589840 | tf_op jit(solution)/shard_map/reduce_scatter | solution.py:93
  283.5 116.4 %reduce-scatter.6.cloned.1.call-done = f32[32,3,3,512]{3,0,2,1:T(8,128)} async-done(((f32[512,3,3,512]{3,0,2,1:T(8,128)}), f32[32,3,3,512]{3,0,2,1:T(8,128)}) %reduce-scatter.6.cloned.1.call-update) | async-done | bytes 589840 | tf_op jit(solution)/shard_map/reduce_scatter | solution.py:92
  (60 shorter events, 14.1 us)
Async XLA Ops:
  7.2 74.7 %copy-start = (bf16[512,8]{0,1:T(8,128)(2,1)S(1)}, bf16[512,8]{0,1:T(8,128)(2,1)}, u32[]{:S(2)}) copy-start(bf16[512,8]{0,1:T(8,128)(2,1)} %param.9) | copy-start | bytes 24580
  7.2 10.0 %copy-start.2 = (bf16[2,256,512]{2,1,0:T(8,128)(2,1)S(1)}, bf16[2,256,512]{2,1,0:T(8,128)(2,1)}, u32[]{:S(2)}) copy-start(bf16[2,256,512]{2,1,0:T(8,128)(2,1)} %param.5) | copy-start | bytes 1572868
  7.2 174.3 %reduce-scatter.10.cloned.1.call-start = ((), (), s32[]{:S(2)}) async-start(), calls=%async_computation.5 | async-start | bytes 278528
  7.2 4.5 %collective-permute-start = (bf16[2,256,512]{2,1,0:T(8,128)(2,1)}, bf16[2,256,512]{2,1,0:T(8,128)(2,1)S(1)}, u32[]{:S(2)}, u32[]{:S(2)}) collective-permute-start(bf16[2,256,512]{2,1,0:T(8,128)(2,1)} %param.5), channel_id=1, source_target_pairs={{0,1},{1,2},{2,3},{3,4},{4,5},{5,6},{6,7},{7,8},{8,9},{9,10},{10,1... | collective-permute-start | bytes 1572872 | tf_op jit(solution)/shard_map/ppermute | solution.py:12
  9.8 6.1 %collective-permute-start.1 = (bf16[2,256,512]{2,1,0:T(8,128)(2,1)}, bf16[2,256,512]{2,1,0:T(8,128)(2,1)S(1)}, u32[]{:S(2)}, u32[]{:S(2)}) collective-permute-start(bf16[2,256,512]{2,1,0:T(8,128)(2,1)} %param.5), channel_id=1, source_target_pairs={{1,0},{2,1},{3,2},{4,3},{5,4},{6,5},{7,6},{8,7},{9,8},{10,9},{11,1... | collective-permute-start | bytes 1572872 | tf_op jit(solution)/shard_map/ppermute | solution.py:15
  76.7 2.2 slice-start
  77.9 1.3 slice-start.1
  81.8 0.8 copy-start.3
  100.4 9.5 %copy-start.4 = (bf16[2,256,512]{2,1,0:T(8,128)(2,1)S(1)}, bf16[2,256,512]{2,1,0:T(8,128)(2,1)}, u32[]{:S(2)}) copy-start(bf16[2,256,512]{2,1,0:T(8,128)(2,1)} %copy.40) | copy-start | bytes 1572868
  100.5 183.0 %reduce-scatter.8.cloned.1.call-start = ((), (), s32[]{:S(2)}) async-start(), calls=%async_computation.4 | async-start | bytes 10027008 | tf_op jit(solution)/shard_map/reduce_scatter | solution.py:93
  129.5 270.3 %reduce-scatter.6.cloned.1.call-start = ((), (), s32[]{:S(2)}) async-start(), calls=%async_computation.3 | async-start | bytes 10027008 | tf_op jit(solution)/shard_map/reduce_scatter | solution.py:92
  139.3 15.1 %collective-permute-start.3 = (bf16[1,256,512]{2,1,0:T(8,128)(2,1)S(1)}, bf16[1,256,512]{2,1,0:T(8,128)(2,1)S(1)}, u32[]{:S(2)}, u32[]{:S(2)}) collective-permute-start(bf16[1,256,512]{2,1,0:T(8,128)(2,1)S(1)} %get-tuple-element.22), channel_id=1, source_target_pairs={{1,0},{2,1},{3,2},{4,3},{5,4},{6,5},{7,6},{8,7},{9,8},{10,9},{11,1... | collective-permute-start | bytes 786440 | tf_op jit(solution)/shard_map/ppermute | solution.py:15
  140.6 13.8 %collective-permute-start.2 = (bf16[1,256,512]{2,1,0:T(8,128)(2,1)S(1)}, bf16[1,256,512]{2,1,0:T(8,128)(2,1)S(1)}, u32[]{:S(2)}, u32[]{:S(2)}) collective-permute-start(bf16[1,256,512]{2,1,0:T(8,128)(2,1)S(1)} %get-tuple-element.21), channel_id=1, source_target_pairs={{0,1},{1,2},{2,3},{3,4},{4,5},{5,6},{6,7},{7,8},{8,9},{9,10},{10,1... | collective-permute-start | bytes 786440 | tf_op jit(solution)/shard_map/ppermute | solution.py:12
  155.6 2.1 copy-start.5
  181.4 218.4 %copy-start.1 = (bf16[512,8]{0,1:T(8,128)(2,1)S(1)}, bf16[512,8]{0,1:T(8,128)(2,1)}, u32[]{:S(2)}) copy-start(bf16[512,8]{0,1:T(8,128)(2,1)} %param.9) | copy-start | bytes 24580
Sparse Core Ops, SparseCore 0:
  100.6 67.7 reduce-scatter.9
  173.0 110.3 reduce-scatter.7
  288.7 111.0 reduce-scatter.5
where the time goes:
time: 408 us; the launch traced here: 406 us
  waiting for transfers between devices  220 us (54%)
  local copies, waits for them, and re-layouts  116 us (28%)
  matrix products  34.7 us (9%)
  starting transfers between devices  17.5 us (4%)
  between operations  14.1 us (3%)
    reduce_scatter x1, waiting for transfers between devices, per_device(): lax.psum_scatter(one_term, 'row', scatter_dimension=0, tiled=True)  116 us
    reduce_scatter x1, waiting for transfers between devices, per_device(): lax.psum_scatter(two_term, 'row', scatter_dimension=0, tiled=True)  101 us
    unnamed x52, local copies, waits for them, and re-layouts  45 us
    slice x11, local copies, waits for them, and re-layouts, gather_taps(): pieces.append(padded[tap_a:tap_a + out_rows, tap_b:tap_b + width])  22.1 us
    dot_general x2, matrix products, grad_term(): jnp.einsum('ptc,pd->ctd', tap_values, cotan_flat, preferred_element_type=...  21.5 us
    reshape x2, local copies, waits for them, and re-layouts, grad_term(): return term.reshape(chans, 3, 3, cotan_flat.shape[1])  19.3 us
    another operation x5, local copies, waits for them, and re-layouts, gather_taps(): stacked = jnp.stack(pieces, axis=2)  18.6 us
    ppermute x2, starting transfers between devices, extended(): lax.ppermute(lax.slice_in_dim(block, block.shape[dim] - width, None, axis...  14.8 us
  transfers between devices with their start and end apart: 7, of which 3 were waited for; matrix products, arithmetic and copies ran while one was open for 17% of the time, Pallas kernels for 0%

commit v1 on v0

v1 whole, which is shorter than its diff:
```python
import functools
import math

import jax
import jax.numpy as jnp
from jax import lax
from jax.experimental import pallas as pl
from jax.experimental.pallas import tpu as pltpu
from jax.sharding import PartitionSpec as P

MESH = pl.DeviceIdType.MESH
F32 = jnp.float32
BF16 = jnp.bfloat16
NT = (((1,), (1,)), ((), ()))
TN = (((0,), (0,)), ((), ()))

X_UP, X_DOWN, D_UP, D_DOWN = 0, 1, 2, 3
D_A, E_A = 4, 7
H_A, F_A = 10, 13
H_LOW, H_HIGH, F_LOW, F_HIGH = 16, 19, 22, 25
HEAD_A = 28
FIXED = 31


def merge(block):
    lead, sub, lanes = math.prod(block.shape[:-2]), block.shape[-2], block.shape[-1]
    if sub % 16 == 0:
        return block.reshape(lead * sub, lanes)
    return block.astype(F32).reshape(lead * sub, lanes).astype(BF16)


def shifts(row):
    wide = row.astype(F32)
    width = wide.shape[0]
    at = lax.broadcasted_iota(jnp.int32, wide.shape, 0)
    before = jnp.where(at == 0, 0.0, pltpu.roll(wide, 1, 0)).astype(BF16)
    after = jnp.where(at == width - 1, 0.0, pltpu.roll(wide, width - 1, 0)).astype(BF16)
    return before, after


def body(
    count, scale,
    feat, onehot, k1_hbm, k2_hbm, head,
    out, g1_out, g2_out, gh_out,
    x, x3, k1, k2, h4, ft, ht, fq, hq, l3, dq, eq, dlow, dhigh, db, d4,
    g1, g2, r1, r2, acc, gh, ghm, ghz,
    send, recv, local,
):
    width, chans = feat.shape[1], feat.shape[2]
    quads = count // 4
    part = chans // count
    me = lax.axis_index("row")
    p, q = me % 4, me // 4
    mate = {1: p + 1 - 2 * (p % 2), 2: (p + 2) % 4, 3: 3 - p}
    has_low, has_high = me > 0, me < count - 1

    def remote(src, dst, slot, row):
        return pltpu.make_async_remote_copy(
            src_ref=src, dst_ref=dst, send_sem=send.at[slot], recv_sem=recv.at[slot],
            device_id={"row": row}, device_id_type=MESH,
        )

    load_x = pltpu.make_async_copy(feat, x.at[pl.ds(2, 2)], local.at[0])
    load_k1 = pltpu.make_async_copy(k1_hbm, k1, local.at[1])
    load_k2 = pltpu.make_async_copy(k2_hbm, k2, local.at[2])
    load_x.start()
    load_k1.start()
    load_k2.start()

    barrier = pltpu.get_barrier_semaphore()

    def greet(row):
        pl.semaphore_signal(barrier, inc=1, device_id={"row": row}, device_id_type=MESH)

    for k in (1, 2, 3):
        greet(4 * q + mate[k])
    for k in range(1, quads):
        greet(4 * ((q + k) % quads) + p)

    @pl.when(has_low)
    def _():
        greet(me - 1)

    @pl.when(has_high)
    def _():
        greet(me + 1)

    sides = (me + count - 1) // count + (2 * count - 2 - me) // count
    pl.semaphore_wait(barrier, quads + 2 + sides)

    x_up = remote(feat, x.at[pl.ds(0, 2)], X_UP, me + 1)
    x_down = remote(feat, x.at[pl.ds(4, 2)], X_DOWN, me - 1)

    @pl.when(has_high)
    def _():
        x_up.start()

    @pl.when(has_low)
    def _():
        x_down.start()

    def fill_x3(row, value):
        before, after = shifts(value)
        rows = pl.ds(row * width, width)
        x3[rows, 0:chans] = before
        x3[rows, chans : 2 * chans] = value
        x3[rows, 2 * chans : 3 * chans] = after

    load_x.wait()
    fill_x3(2, x[2])
    fill_x3(3, x[3])

    @pl.when(has_low)
    def _():
        x_up.wait_recv()

    @pl.when(jnp.logical_not(has_low))
    def _():
        x[0:2] = jnp.zeros((2, width, chans), BF16)

    fill_x3(0, x[0])
    fill_x3(1, x[1])

    @pl.when(has_high)
    def _():
        x_down.wait_recv()

    @pl.when(jnp.logical_not(has_high))
    def _():
        x[4:6] = jnp.zeros((2, width, chans), BF16)

    fill_x3(4, x[4])
    fill_x3(5, x[5])

    def conv(rows, kernel):
        size = rows * width
        for a in range(3):
            term = jnp.dot(
                x3[a * width : a * width + size, :],
                kernel[a].reshape(3 * chans, chans),
                preferred_element_type=F32,
            )
            if a == 0:
                acc[0:size, :] = term
            else:
                acc[0:size, :] += term

    load_k1.wait()
    conv(4, k1)
    for row in range(4):
        value = jnp.maximum(acc[row * width : (row + 1) * width, :], 0.0)
        if row == 0:
            value = value * has_low.astype(F32)
        if row == 3:
            value = value * has_high.astype(F32)
        h4[row] = value.astype(BF16)

    def transpose_rows(source, first, target):
        for row in range(4):
            flipped = jnp.transpose(source[first + row].astype(F32))
            target[row] = flipped.reshape(quads, 4, part, width).astype(BF16)

    def spread(source, target, slot, low_slot, high_slot, sem):
        own = pltpu.make_async_copy(
            source.at[pl.ds(1, 2), :, p], target.at[pl.ds(1 + 2 * p, 2)], local.at[sem]
        )
        own.start()
        mids, lows, highs = [], [], []
        for k in (1, 2, 3):
            mids.append(remote(
                source.at[pl.ds(1, 2), :, mate[k]], target.at[pl.ds(1 + 2 * p, 2)],
                slot + k - 1, 4 * q + mate[k],
            ))
            lows.append(remote(
                source.at[pl.ds(0, 1), :, mate[k]], target.at[pl.ds(0, 1)],
                low_slot + k - 1, 4 * q + mate[k],
            ))
            highs.append(remote(
                source.at[pl.ds(3, 1), :, mate[k]], target.at[pl.ds(9, 1)],
                high_slot + k - 1, 4 * q + mate[k],
            ))
        low_own = pltpu.make_async_copy(
            source.at[pl.ds(0, 1), :, p], target.at[pl.ds(0, 1)], local.at[sem + 1]
        )
        high_own = pltpu.make_async_copy(
            source.at[pl.ds(3, 1), :, p], target.at[pl.ds(9, 1)], local.at[sem + 2]
        )
        for copy in mids:
            copy.start()

        @pl.when(p == 0)
        def _():
            low_own.start()
            for copy in lows:
                copy.start()

        @pl.when(p == 3)
        def _():
            high_own.start()
            for copy in highs:
                copy.start()

        def wait_in():
            own.wait()
            for copy in mids:
                copy.wait_recv()

            @pl.when(p == 0)
            def _():
                low_own.wait()

            @pl.when(p == 3)
            def _():
                high_own.wait()

            for k in (1, 2, 3):
                @pl.when(p == k)
                def _():
                    lows[k - 1].wait_recv()

                @pl.when(p == 3 - k)
                def _():
                    highs[k - 1].wait_recv()

        def wait_out():
            for copy in mids:
                copy.wait_send()

            @pl.when(p == 0)
            def _():
                for copy in lows:
                    copy.wait_send()

            @pl.when(p == 3)
            def _():
                for copy in highs:
                    copy.wait_send()

        return wait_in, wait_out

    transpose_rows(h4, 0, ht)
    h_in, h_sent = spread(ht, hq, H_A, H_LOW, H_HIGH, 3)

    for row in range(4):
        fill_x3(row, h4[row])
    load_k2.wait()
    conv(2, k2)
    section = jnp.maximum(acc[0 : 2 * width, :], 0.0).astype(BF16)
    out[...] = section.reshape(2, width, chans)
    logits = lax.dot_general(section, head[...], NT, preferred_element_type=F32)
    dlogits = ((logits - onehot[...]) * scale).astype(BF16)
    dout = jnp.dot(dlogits, head[...], preferred_element_type=F32)
    dout = jnp.where(section.astype(F32) > 0, dout, 0.0).astype(BF16)
    mine = pl.ds(2 * p, 2)
    dq[mine] = dout.reshape(2, width, chans)

    d_up = remote(dq.at[pl.ds(2 * p + 1, 1)], dlow, D_UP, me + 1)
    d_down = remote(dq.at[pl.ds(2 * p, 1)], dhigh, D_DOWN, me - 1)

    @pl.when(has_high)
    def _():
        d_up.start()

    @pl.when(has_low)
    def _():
        d_down.start()

    def gather(buffer, slot):
        near = remote(buffer.at[mine], buffer.at[mine], slot, 4 * q + mate[1])
        far = remote(buffer.at[mine], buffer.at[mine], slot + 1, 4 * q + mate[2])
        theirs = pl.ds(2 * mate[2], 2)
        passed = remote(buffer.at[theirs], buffer.at[theirs], slot + 2, 4 * q + mate[1])
        far.start()
        near.start()
        return near, far, passed

    d_near, d_far, d_passed = gather(dq, D_A)

    gh[...] = lax.dot_general(dlogits, section, TN, preferred_element_type=F32)
    heads = []
    for k in (1, 2, 3):
        copy = remote(gh, ghm.at[k - 1], HEAD_A + k - 1, 4 * q + mate[k])
        copy.start()
        heads.append(copy)
    transpose_rows(x, 1, ft)
    f_in, f_sent = spread(ft, fq, F_A, F_LOW, F_HIGH, 6)

    def fill_d4(row, value):
        before, after = shifts(value)
        rows = pl.ds(row * width, width)
        d4[0, rows, :] = after
        d4[1, rows, :] = value
        d4[2, rows, :] = before

    fill_d4(1, dq[2 * p])
    fill_d4(2, dq[2 * p + 1])

    @pl.when(has_low)
    def _():
        d_up.wait_recv()

    @pl.when(jnp.logical_not(has_low))
    def _():
        dlow[...] = jnp.zeros((1, width, chans), BF16)

    fill_d4(0, dlow[0])

    @pl.when(has_high)
    def _():
        d_down.wait_recv()

    @pl.when(jnp.logical_not(has_high))
    def _():
        dhigh[...] = jnp.zeros((1, width, chans), BF16)

    fill_d4(3, dhigh[0])

    two = 2 * width
    for a in range(3):
        for b in range(3):
            term = lax.dot_general(
                d4[b, (2 - a) * width : (2 - a) * width + two, :], k2[a, b], NT,
                preferred_element_type=F32,
            )
            if a == 0 and b == 0:
                acc[0:two, :] = term
            else:
                acc[0:two, :] += term
    hidden = h4[1:3].reshape(two, chans).astype(F32)
    dhidden = jnp.where(hidden > 0, acc[0:two, :], 0.0).astype(BF16)
    eq[mine] = dhidden.reshape(2, width, chans)
    e_near, e_far, e_passed = gather(eq, E_A)

    def fill_l3(source):
        for row in range(8):
            l3[:, row * width : (row + 1) * width] = merge(source[row : row + 3])

    def fill_db(buffer, block):
        for row in range(2):
            before, after = shifts(buffer[2 * block + row])
            rows = pl.ds(pl.multiple_of((2 * block + row) * width, width), width)
            db[0, rows, :] = after
            db[1, rows, :] = before

    def kernel_grad(buffer, target):
        for b in range(3):
            if b == 1:
                rhs = buffer[...].reshape(8 * width, chans)
            else:
                rhs = db[b // 2]
            term = jnp.dot(l3[...], rhs, preferred_element_type=F32)
            term = term.reshape(3, quads, part, chans)
            for other in range(quads):
                target[other, :, b] = term[:, other].astype(BF16)

    def scatter(source, landing, slot):
        copies = []
        for k in range(1, quads):
            other = (q + k) % quads
            copy = remote(source.at[other], landing.at[k - 1], slot + k - 1, 4 * other + p)
            copy.start()
            copies.append(copy)
        return copies

    def grad_stage(spread_in, source, copies, buffer, target, landing, slot):
        near, far, passed = copies
        fill_db(buffer, p)
        far.wait_recv()
        passed.start()
        spread_in()
        fill_l3(source)
        near.wait_recv()
        fill_db(buffer, mate[1])
        fill_db(buffer, mate[2])
        passed.wait_recv()
        fill_db(buffer, mate[3])
        kernel_grad(buffer, target)
        return scatter(target, landing, slot)

    s2 = grad_stage(h_in, hq, (d_near, d_far, d_passed), dq, g2, r2, FIXED)
    s1 = grad_stage(f_in, fq, (e_near, e_far, e_passed), eq, g1, r1, FIXED + quads - 1)

    for copy in heads:
        copy.wait_recv()
        copy.wait_send()
    gh[...] = gh[...] + ghm[0] + ghm[1] + ghm[2]
    zs = []
    for k in range(1, quads):
        copy = remote(
            gh, ghz.at[k - 1], FIXED + 2 * (quads - 1) + k - 1, 4 * ((q + k) % quads) + p
        )
        copy.start()
        zs.append(copy)

    def finish(copies, source, landing, target):
        for copy in copies:
            copy.wait_recv()
        for a in range(3):
            total = source[q, a].astype(F32)
            for k in range(quads - 1):
                total = total + landing[k, a].astype(F32)
            target[a] = total

    finish(s2, g2, r2, g2_out)
    total = gh[...]
    for k, copy in enumerate(zs):
        copy.wait_recv()
        total = total + ghz[k]
    gh_out[...] = total
    finish(s1, g1, r1, g1_out)

    @pl.when(has_high)
    def _():
        x_up.wait_send()
        d_up.wait_send()

    @pl.when(has_low)
    def _():
        x_down.wait_send()
        d_down.wait_send()

    h_sent()
    f_sent()
    for copy in (d_near, d_far, d_passed, e_near, e_far, e_passed, *s1, *s2, *zs):
        copy.wait_send()


def per_device(features, labels, kernel_one, kernel_two, head_weight):
    rows, width, chans = features.shape
    classes = head_weight.shape[1]
    count = lax.axis_size("row")
    quads, part = count // 4, chans // count
    scale = 1.0 / math.sqrt(rows * count * width)
    onehot = (labels.reshape(-1)[:, None] == jnp.arange(classes, dtype=jnp.int32)[None, :]).astype(
        F32
    )
    slots = FIXED + 3 * (quads - 1)
    vmem = pl.BlockSpec(memory_space=pltpu.VMEM)
    hbm = pl.BlockSpec(memory_space=pl.ANY)
    scratch = [
        pltpu.VMEM((6, width, chans), BF16),
        pltpu.VMEM((6 * width, 3 * chans), BF16),
        pltpu.VMEM((3, 3, chans, chans), BF16),
        pltpu.VMEM((3, 3, chans, chans), BF16),
        pltpu.VMEM((4, width, chans), BF16),
        pltpu.VMEM((4, quads, 4, part, width), BF16),
        pltpu.VMEM((4, quads, 4, part, width), BF16),
        pltpu.VMEM((10, quads, part, width), BF16),
        pltpu.VMEM((10, quads, part, width), BF16),
        pltpu.VMEM((3 * quads * part, 8 * width), BF16),
        pltpu.VMEM((8, width, chans), BF16),
        pltpu.VMEM((8, width, chans), BF16),
        pltpu.VMEM((1, width, chans), BF16),
        pltpu.VMEM((1, width, chans), BF16),
        pltpu.VMEM((2, 8 * width, chans), BF16),
        pltpu.VMEM((3, 4 * width, chans), BF16),
        pltpu.VMEM((quads, 3, 3, part, chans), BF16),
        pltpu.VMEM((quads, 3, 3, part, chans), BF16),
        pltpu.VMEM((quads - 1, 3, 3, part, chans), BF16),
        pltpu.VMEM((quads - 1, 3, 3, part, chans), BF16),
        pltpu.VMEM((4 * width, chans), F32),
        pltpu.VMEM((classes, chans), F32),
        pltpu.VMEM((3, classes, chans), F32),
        pltpu.VMEM((quads - 1, classes, chans), F32),
        pltpu.SemaphoreType.DMA((slots,)),
        pltpu.SemaphoreType.DMA((slots,)),
        pltpu.SemaphoreType.DMA((9,)),
    ]
    section_out, one, two, head_t = pl.pallas_call(
        functools.partial(body, count, scale),
        out_shape=(
            jax.ShapeDtypeStruct((rows, width, chans), BF16),
            jax.ShapeDtypeStruct((3, 3, part, chans), F32),
            jax.ShapeDtypeStruct((3, 3, part, chans), F32),
            jax.ShapeDtypeStruct((classes, chans), F32),
        ),
        in_specs=[hbm, vmem, hbm, hbm, vmem],
        out_specs=(vmem, vmem, vmem, vmem),
        scratch_shapes=scratch,
        compiler_params=pltpu.CompilerParams(
            collective_id=0, has_side_effects=True, vmem_limit_bytes=60 * 2**20
        ),
    )(features, onehot, kernel_one, kernel_two, head_weight.T)
    head_block = lax.dynamic_slice_in_dim(head_t, lax.axis_index("row") * part, part, axis=1)
    return (
        section_out,
        jnp.transpose(one, (2, 0, 1, 3)),
        jnp.transpose(two, (2, 0, 1, 3)),
        head_block.T,
    )


def solution(mesh):
    placed = (P(("groups", "row"), None, None), P(("groups", "row"), None), P(), P(), P())
    return jax.shard_map(
        per_device,
        mesh=mesh,
        in_specs=placed,
        out_specs=(
            P(("groups", "row"), None, None),
            P(("groups", "row"), None, None, None),
            P(("groups", "row"), None, None, None),
            P(("groups", "row"), None),
        ),
        check_vma=False,
    )
```

time: 408 us -> 119 us (0.29)
  waiting for transfers between devices: 220 us -> 0 us
  Pallas kernels: 0 us -> 109 us
  local copies, waits for them, and re-layouts: 116 us -> 7.73 us
  matrix products: 34.7 us -> 0 us
  starting transfers between devices: 17.5 us -> 0 us
  between operations: 14.1 us -> 0.65 us
    reduce_scatter x2 -> x0, waiting for transfers between devices: 217 us -> none  [the longest x1 116 us: per_device(): lax.psum_scatter(one_term, 'row', scatter_dimension=0, tiled=True)]
    pallas_call x0 -> x1, Pallas kernels: none -> 109 us  [per_device(): pl.pallas_call(functools.partial(body, count, scale), out_shape=(jax.Shap...]
    unnamed x52 -> x4, local copies, waits for them, and re-layouts: 45 us -> 6.38 us
    dot_general x6 -> x0, matrix products: 33.7 us -> none  [the longest x2 21.5 us: grad_term(): jnp.einsum('ptc,pd->ctd', tap_values, cotan_flat, preferred_element_type=...]
    slice x13 -> x0, local copies, waits for them, and re-layouts: 27 us -> none  [the longest x11 22.1 us: gather_taps(): pieces.append(padded[tap_a:tap_a + out_rows, tap_b:tap_b + width])]
    reshape x3 -> x0, local copies, waits for them, and re-layouts: 20 us -> none  [the longest x2 19.3 us: grad_term(): return term.reshape(chans, 3, 3, cotan_flat.shape[1])]
    another operation x5 -> x0, local copies, waits for them, and re-layouts: 18.6 us -> none  [gather_taps(): stacked = jnp.stack(pieces, axis=2)]
    ppermute x4 -> x0, starting transfers between devices: 17.3 us -> none  [the longest x2 14.8 us: extended(): lax.ppermute(lax.slice_in_dim(block, block.shape[dim] - width, None, axis...]
  transfers between devices with their start and end apart: 7 -> 0, of which waited for: 3 -> 0; matrix products, arithmetic and copies ran while one was open for 17% -> 0% of each run, Pallas kernels for 0% -> 0%
where the time goes in v1:
time: 119 us
  Pallas kernels  109 us (92%)
  local copies, waits for them, and re-layouts  7.73 us (6%)
    pallas_call x1, Pallas kernels, per_device(): pl.pallas_call(functools.partial(body, count, scale), out_shape=(jax.Shap...  109 us
    unnamed x4, local copies, waits for them, and re-layouts  6.38 us

profile of v1, /device:TPU:0, one launch (start us, length us, event | category | flops | bytes accessed | tf_op | source)
XLA Modules:
  0.0 118.6 jit_solution(9701308400014292935)
XLA Ops:
  0.6 0.7 copy.9
  1.3 0.8 fusion.onehot
  2.2 109.4 %shard_map.84 = (bf16[2,256,512]{2,1,0:T(8,128)(2,1)}, f32[3,3,32,512]{3,2,1,0:T(8,128)}, f32[3,3,32,512]{3,2,1,0:T(8,128)}, f32[8,512]{1,0:T(8,128)}) custom-call(bf16[2,256,512]{2,1,0:T(8,128)(2,1)} %feat.1, f32[512,8]{1,0:T(8,128)} %fusion.onehot, bf16[3,3,512,512]{3,2,1,0:T(8,128)(2,1)} %k1_hbm.1, bf16[3,3,512,512]{3,2,1,0:T(8,128)(2,1)} %k2_hbm.1, ...), custom_call_target="tpu_custom_call" | custom-call | tf_op jit(solution)/shard_map/pallas_call | solution.py:469
  111.6 1.3 %dynamic-slice_bitcast_fusion = f32[32,8]{0,1:T(8,128)} fusion(f32[8,512]{1,0:T(8,128)} %get-tuple-element.11, s32[]{:T(128)S(6)} %select_n.3), kind=kLoop, calls=%fused_computation.2 | loop fusion | bytes 2052 | tf_op jit(solution)/shard_map/transpose | solution.py:489
  112.9 1.9 %copy.13 = bf16[2,256,512]{2,1,0:T(8,128)(2,1)} copy(bf16[2,256,512]{2,1,0:T(8,128)(2,1)} %get-tuple-element.16) | data formatting | bytes 1048576
  114.8 1.9 %copy.14 = f32[32,3,3,512]{3,0,2,1:T(8,128)} copy(f32[32,3,3,512]{3,0,2,1:T(8,128)} %bitcast.8) | data formatting | bytes 1179648
  116.7 1.9 %copy.15 = f32[32,3,3,512]{3,0,2,1:T(8,128)} copy(f32[32,3,3,512]{3,0,2,1:T(8,128)} %bitcast.7) | data formatting | bytes 1179648

commit v2 on v1

--- a/solution.py
+++ b/solution.py
@@ -43,7 +43,7 @@
     feat, onehot, k1_hbm, k2_hbm, head,
     out, g1_out, g2_out, gh_out,
     x, x3, k1, k2, h4, ft, ht, fq, hq, l3, dq, eq, dlow, dhigh, db, d4,
-    g1, g2, r1, r2, acc, gh, ghm, ghz,
+    g1, g2, m1, m2, c1, c2, r1, r2, acc, gh, ghm, ghz,
     send, recv, local,
 ):
     width, chans = feat.shape[1], feat.shape[2]
@@ -342,7 +342,12 @@
             db[0, rows, :] = after
             db[1, rows, :] = before
 
-    def kernel_grad(buffer, target):
+    half = quads // 2
+    side, pair = q % 2, q // 2
+    twin = 4 * (q + 1 - 2 * side) + p
+
+    def kernel_grad(buffer, target, met, slot):
+        copies = []
         for b in range(3):
             if b == 1:
                 rhs = buffer[...].reshape(8 * width, chans)
@@ -351,18 +356,30 @@
             term = jnp.dot(l3[...], rhs, preferred_element_type=F32)
             term = term.reshape(3, quads, part, chans)
             for other in range(quads):
-                target[other, :, b] = term[:, other].astype(BF16)
-
-    def scatter(source, landing, slot):
-        copies = []
-        for k in range(1, quads):
-            other = (q + k) % quads
-            copy = remote(source.at[other], landing.at[k - 1], slot + k - 1, 4 * other + p)
+                target[other % 2, other // 2, b] = term[:, other].astype(BF16)
+            copy = remote(target.at[1 - side, :, b], met.at[b], slot + b, twin)
             copy.start()
             copies.append(copy)
         return copies
 
-    def grad_stage(spread_in, source, copies, buffer, target, landing, slot):
+    def combine(copies, target, met, joined, landing, slot):
+        sent = []
+        for b in range(3):
+            copies[b].wait_recv()
+            for other in range(half):
+                total = target[side, other, b].astype(F32) + met[b, other].astype(F32)
+                joined[b, other] = total.astype(BF16)
+            for k in range(1, half):
+                goal = (pair + k) % half
+                copy = remote(
+                    joined.at[b, goal], landing.at[k - 1, b],
+                    slot + 3 + 3 * (k - 1) + b, 4 * (2 * goal + side) + p,
+                )
+                copy.start()
+                sent.append(copy)
+        return sent
+
+    def grad_stage(spread_in, source, copies, buffer, target, met, slot):
         near, far, passed = copies
         fill_db(buffer, p)
         far.wait_recv()
@@ -374,11 +391,13 @@
         fill_db(buffer, mate[2])
         passed.wait_recv()
         fill_db(buffer, mate[3])
-        kernel_grad(buffer, target)
-        return scatter(target, landing, slot)
-
-    s2 = grad_stage(h_in, hq, (d_near, d_far, d_passed), dq, g2, r2, FIXED)
-    s1 = grad_stage(f_in, fq, (e_near, e_far, e_passed), eq, g1, r1, FIXED + quads - 1)
+        return kernel_grad(buffer, target, met, slot)
+
+    per_grad = 3 * half
+    m2_copies = grad_stage(h_in, hq, (d_near, d_far, d_passed), dq, g2, m2, FIXED)
+    m1_copies = grad_stage(f_in, fq, (e_near, e_far, e_passed), eq, g1, m1, FIXED + per_grad)
+    s2 = combine(m2_copies, g2, m2, c2, r2, FIXED)
+    s1 = combine(m1_copies, g1, m1, c1, r1, FIXED + per_grad)
 
     for copy in heads:
         copy.wait_recv()
@@ -387,27 +406,27 @@
     zs = []
     for k in range(1, quads):
         copy = remote(
-            gh, ghz.at[k - 1], FIXED + 2 * (quads - 1) + k - 1, 4 * ((q + k) % quads) + p
+            gh, ghz.at[k - 1], FIXED + 2 * per_grad + k - 1, 4 * ((q + k) % quads) + p
         )
         copy.start()
         zs.append(copy)
 
-    def finish(copies, source, landing, target):
+    def finish(copies, source, met, landing, target):
         for copy in copies:
             copy.wait_recv()
-        for a in range(3):
-            total = source[q, a].astype(F32)
-            for k in range(quads - 1):
-                total = total + landing[k, a].astype(F32)
-            target[a] = total
-
-    finish(s2, g2, r2, g2_out)
+        for b in range(3):
+            total = source[side, pair, b].astype(F32) + met[b, pair].astype(F32)
+            for k in range(half - 1):
+                total = total + landing[k, b].astype(F32)
+            target[:, b] = total
+
+    finish(s2, g2, m2, r2, g2_out)
     total = gh[...]
     for k, copy in enumerate(zs):
         copy.wait_recv()
         total = total + ghz[k]
     gh_out[...] = total
-    finish(s1, g1, r1, g1_out)
+    finish(s1, g1, m1, r1, g1_out)
 
     @pl.when(has_high)
     def _():
@@ -421,7 +440,7 @@
 
     h_sent()
     f_sent()
-    for copy in (d_near, d_far, d_passed, e_near, e_far, e_passed, *s1, *s2, *zs):
+    for copy in (d_near, d_far, d_passed, e_near, e_far, e_passed, *s1, *s2, *zs, *m1_copies, *m2_copies):
         copy.wait_send()
 
 
@@ -434,7 +453,7 @@
     onehot = (labels.reshape(-1)[:, None] == jnp.arange(classes, dtype=jnp.int32)[None, :]).astype(
         F32
     )
-    slots = FIXED + 3 * (quads - 1)
+    slots = FIXED + 3 * quads + quads - 1
     vmem = pl.BlockSpec(memory_space=pltpu.VMEM)
     hbm = pl.BlockSpec(memory_space=pl.ANY)
     scratch = [
@@ -454,10 +473,14 @@
         pltpu.VMEM((1, width, chans), BF16),
         pltpu.VMEM((2, 8 * width, chans), BF16),
         pltpu.VMEM((3, 4 * width, chans), BF16),
-        pltpu.VMEM((quads, 3, 3, part, chans), BF16),
-        pltpu.VMEM((quads, 3, 3, part, chans), BF16),
-        pltpu.VMEM((quads - 1, 3, 3, part, chans), BF16),
-        pltpu.VMEM((quads - 1, 3, 3, part, chans), BF16),
+        pltpu.VMEM((2, quads // 2, 3, 3, part, chans), BF16),
+        pltpu.VMEM((2, quads // 2, 3, 3, part, chans), BF16),
+        pltpu.VMEM((3, quads // 2, 3, part, chans), BF16),
+        pltpu.VMEM((3, quads // 2, 3, part, chans), BF16),
+        pltpu.VMEM((3, quads // 2, 3, part, chans), BF16),
+        pltpu.VMEM((3, quads // 2, 3, part, chans), BF16),
+        pltpu.VMEM((quads // 2 - 1, 3, 3, part, chans), BF16),
+        pltpu.VMEM((quads // 2 - 1, 3, 3, part, chans), BF16),
         pltpu.VMEM((4 * width, chans), F32),
         pltpu.VMEM((classes, chans), F32),
         pltpu.VMEM((3, classes, chans), F32),

time: 119 us -> 109 us (0.916)
  Pallas kernels: 109 us -> 99.7 us
    pallas_call x1, Pallas kernels: 109 us -> 99.7 us  [per_device(): pl.pallas_call(functools.partial(body, count, scale), out_shape=(jax.Shap...]
where the time goes in v2:
time: 109 us
  Pallas kernels  99.7 us (91%)
  local copies, waits for them, and re-layouts  7.73 us (7%)
    pallas_call x1, Pallas kernels, per_device(): pl.pallas_call(functools.partial(body, count, scale), out_shape=(jax.Shap...  99.7 us
    unnamed x4, local copies, waits for them, and re-layouts  6.38 us

profile of v2, /device:TPU:0, one launch (start us, length us, event | category | flops | bytes accessed | tf_op | source)
XLA Modules:
  0.0 108.9 jit_solution(13596147533534623610)
XLA Ops:
  0.6 0.7 copy.9
  1.3 0.8 fusion.onehot
  2.2 99.7 %shard_map.84 = (bf16[2,256,512]{2,1,0:T(8,128)(2,1)}, f32[3,3,32,512]{3,2,1,0:T(8,128)}, f32[3,3,32,512]{3,2,1,0:T(8,128)}, f32[8,512]{1,0:T(8,128)}) custom-call(bf16[2,256,512]{2,1,0:T(8,128)(2,1)} %feat.1, f32[512,8]{1,0:T(8,128)} %fusion.onehot, bf16[3,3,512,512]{3,2,1,0:T(8,128)(2,1)} %k1_hbm.1, bf16[3,3,512,512]{3,2,1,0:T(8,128)(2,1)} %k2_hbm.1, ...), custom_call_target="tpu_custom_call" | custom-call | tf_op jit(solution)/shard_map/pallas_call | solution.py:492
  101.8 1.3 %dynamic-slice_bitcast_fusion = f32[32,8]{0,1:T(8,128)} fusion(f32[8,512]{1,0:T(8,128)} %get-tuple-element.11, s32[]{:T(128)S(6)} %select_n.3), kind=kLoop, calls=%fused_computation.2 | loop fusion | bytes 2052 | tf_op jit(solution)/shard_map/transpose | solution.py:512
  103.2 1.9 %copy.13 = bf16[2,256,512]{2,1,0:T(8,128)(2,1)} copy(bf16[2,256,512]{2,1,0:T(8,128)(2,1)} %get-tuple-element.16) | data formatting | bytes 1048576
  105.0 1.9 %copy.14 = f32[32,3,3,512]{3,0,2,1:T(8,128)} copy(f32[32,3,3,512]{3,0,2,1:T(8,128)} %bitcast.8) | data formatting | bytes 1179648
  107.0 1.9 %copy.15 = f32[32,3,3,512]{3,0,2,1:T(8,128)} copy(f32[32,3,3,512]{3,0,2,1:T(8,128)} %bitcast.7) | data formatting | bytes 1179648

commit v3 on v2

--- a/solution.py
+++ b/solution.py
@@ -144,16 +144,6 @@
                 acc[0:size, :] = term
             else:
                 acc[0:size, :] += term
-
-    load_k1.wait()
-    conv(4, k1)
-    for row in range(4):
-        value = jnp.maximum(acc[row * width : (row + 1) * width, :], 0.0)
-        if row == 0:
-            value = value * has_low.astype(F32)
-        if row == 3:
-            value = value * has_high.astype(F32)
-        h4[row] = value.astype(BF16)
 
     def transpose_rows(source, first, target):
         for row in range(4):
@@ -238,6 +228,19 @@
 
         return wait_in, wait_out
 
+    transpose_rows(x, 1, ft)
+    f_in, f_sent = spread(ft, fq, F_A, F_LOW, F_HIGH, 6)
+
+    load_k1.wait()
+    conv(4, k1)
+    for row in range(4):
+        value = jnp.maximum(acc[row * width : (row + 1) * width, :], 0.0)
+        if row == 0:
+            value = value * has_low.astype(F32)
+        if row == 3:
+            value = value * has_high.astype(F32)
+        h4[row] = value.astype(BF16)
+
     transpose_rows(h4, 0, ht)
     h_in, h_sent = spread(ht, hq, H_A, H_LOW, H_HIGH, 3)
 
@@ -282,8 +285,6 @@
         copy = remote(gh, ghm.at[k - 1], HEAD_A + k - 1, 4 * q + mate[k])
         copy.start()
         heads.append(copy)
-    transpose_rows(x, 1, ft)
-    f_in, f_sent = spread(ft, fq, F_A, F_LOW, F_HIGH, 6)
 
     def fill_d4(row, value):
         before, after = shifts(value)
@@ -506,7 +507,7 @@
     )(features, onehot, kernel_one, kernel_two, head_weight.T)
     head_block = lax.dynamic_slice_in_dim(head_t, lax.axis_index("row") * part, part, axis=1)
     return (
-        section_out,
+        jnp.maximum(section_out, 0),
         jnp.transpose(one, (2, 0, 1, 3)),
         jnp.transpose(two, (2, 0, 1, 3)),
         head_block.T,

time: 109 us -> 114 us (1.046)
  Pallas kernels: 99.7 us -> 104 us
  other arithmetic: 0.84 us -> 2.71 us
  local copies, waits for them, and re-layouts: 7.73 us -> 5.86 us
    pallas_call x1, Pallas kernels: 99.7 us -> 104 us  [per_device(): pl.pallas_call(functools.partial(body, count, scale), out_shape=(jax.Shap...]
    max x0 -> x1, other arithmetic: none -> 1.87 us  [per_device(): jnp.maximum(section_out, 0)]
    unnamed x4 -> x3, local copies, waits for them, and re-layouts: 6.38 us -> 4.52 us
where the time goes in v3:
time: 114 us
  Pallas kernels  104 us (91%)
  local copies, waits for them, and re-layouts  5.86 us (5%)
  other arithmetic  2.71 us (2%)
    pallas_call x1, Pallas kernels, per_device(): pl.pallas_call(functools.partial(body, count, scale), out_shape=(jax.Shap...  104 us
    unnamed x3, local copies, waits for them, and re-layouts  4.52 us

profile of v3, /device:TPU:0, one launch (start us, length us, event | category | flops | bytes accessed | tf_op | source)
XLA Modules:
  0.0 113.6 jit_solution(11072267995757055219)
XLA Ops:
  0.6 0.7 copy.9
  1.3 0.8 fusion.onehot
  2.2 104.4 %shard_map.84 = (bf16[2,256,512]{2,1,0:T(8,128)(2,1)}, f32[3,3,32,512]{3,2,1,0:T(8,128)}, f32[3,3,32,512]{3,2,1,0:T(8,128)}, f32[8,512]{1,0:T(8,128)}) custom-call(bf16[2,256,512]{2,1,0:T(8,128)(2,1)} %feat.1, f32[512,8]{1,0:T(8,128)} %fusion.onehot, bf16[3,3,512,512]{3,2,1,0:T(8,128)(2,1)} %k1_hbm.1, bf16[3,3,512,512]{3,2,1,0:T(8,128)(2,1)} %k2_hbm.1, ...), custom_call_target="tpu_custom_call" | custom-call | tf_op jit(solution)/shard_map/pallas_call | solution.py:493
  106.5 1.3 %dynamic-slice_bitcast_fusion = f32[32,8]{0,1:T(8,128)} fusion(f32[8,512]{1,0:T(8,128)} %get-tuple-element.11, s32[]{:T(128)S(6)} %select_n.3), kind=kLoop, calls=%fused_computation.3 | loop fusion | bytes 2052 | tf_op jit(solution)/shard_map/transpose | solution.py:513
  107.9 1.9 %broadcast_maximum_fusion = bf16[2,256,512]{2,1,0:T(8,128)(2,1)} fusion(bf16[2,256,512]{2,1,0:T(8,128)(2,1)} %get-tuple-element.8), kind=kLoop, calls=%fused_computation | loop fusion | flops 262144 | bytes 1048576 | tf_op jit(solution)/shard_map/max | solution.py:510
  109.8 1.9 %copy.12 = f32[32,3,3,512]{3,0,2,1:T(8,128)} copy(f32[32,3,3,512]{3,0,2,1:T(8,128)} %bitcast.8) | data formatting | bytes 1179648
  111.7 1.9 %copy.13 = f32[32,3,3,512]{3,0,2,1:T(8,128)} copy(f32[32,3,3,512]{3,0,2,1:T(8,128)} %bitcast.7) | data formatting | bytes 1179648
